TPU v7x, 512 devices: a whole 4x8x8 slice. The times are simulated.
512 devices in a mesh: dp: 32 (over x, z_lo, core), fsdp: 16 (over z_hi, y).
Axes of the slice: x: 4, y: 8, z: 8 (z_hi: 2, z_lo: 4; z = z_hi * 4 + z_lo), core: 2. Of those that a mesh axis runs over, the one named last changes fastest.
Arguments:
- hidden: bfloat16 [4096, 1536], P('dp', 'fsdp'), may hold values from -0.5 to 0.5
- teacher: bfloat16 [4096, 4096], P('dp', 'fsdp'), may hold values from -40 to 40
- projector: bfloat16 [1536, 1536], P('fsdp'), may hold values from -0.15625 to 0.15625
Outputs:
- grad_hidden: float32 [4096, 1536], P('dp', 'fsdp')
- grad_proj: float32 [1536, 1536], P('fsdp')
- loss: float32 [], replicated
All inputs are finite; a program needn't handle non-finite values.
Results may differ from a plain program's by a relative error of at most 0.0085.
The roundings to bfloat16 on the way count: a program that leaves them out, or rounds other values in their place, can miss the bound.
Values may be sent and summed in bfloat16 or wider, within the bound.
No kernel may reach another device: no remote copies, remote signals or barrier semaphores. Data moves between devices by JAX's collectives and lax.ppermute only.
A program may use at most 64 MiB of HBM per device.

v0:
```python
import jax
import jax.numpy as jnp
from jax import lax
from jax.sharding import PartitionSpec as P

EPSILON = 1e-06
HIGHEST = lax.Precision.HIGHEST


def radial_sum(unit_f, grad_unit):
    return lax.psum(jnp.sum(unit_f * grad_unit, axis=1), "fsdp")


def body(hidden, teacher, projector):
    row_count = hidden.shape[0]
    width_local = hidden.shape[1]
    contract = (((1,), (1,)), ((), ()))
    rows_first = (((0,), (0,)), ((), ()))
    width_cross = (((0,), (1,)), ((), ()))
    embed = lax.psum_scatter(
        lax.dot_general(projector, hidden, width_cross, preferred_element_type=jnp.float32),
        "fsdp",
        scatter_dimension=0,
        tiled=True,
    ).T
    teach_f = teacher.astype(jnp.float32)
    sq_student, sq_teacher = lax.psum(
        (jnp.sum(embed * embed, axis=1), jnp.sum(teach_f * teach_f, axis=1)), "fsdp"
    )
    inv_student = lax.rsqrt(sq_student + EPSILON)[:, None]
    unit_f = embed * inv_student
    student = unit_f.astype(jnp.bfloat16)
    target = (teach_f * lax.rsqrt(sq_teacher + EPSILON)[:, None]).astype(jnp.bfloat16)
    upper = jnp.concatenate([student, target], axis=1)
    lower = jnp.concatenate([student, -target], axis=1)
    lower_all = lax.all_gather(lower, "dp", axis=0, tiled=True)
    partial_value = lax.dot_general(upper, lower_all, contract, preferred_element_type=jnp.float32)
    differ = lax.psum(partial_value, "fsdp")
    squares = jnp.sum(differ * differ)
    grad_unit = 4.0 * jnp.dot(
        differ,
        lower_all[:, :width_local].astype(jnp.float32),
        precision=HIGHEST,
        preferred_element_type=jnp.float32,
    )
    radial = radial_sum(unit_f, grad_unit)
    grad_embed = (inv_student * (grad_unit - unit_f * radial[:, None])).astype(jnp.bfloat16)
    piece = lax.all_gather(grad_embed, "fsdp", axis=1, tiled=True)
    hidden_acc = lax.dot_general(piece, projector, contract, preferred_element_type=jnp.float32)
    proj_piece = lax.dot_general(hidden, piece, rows_first, preferred_element_type=jnp.float32)
    grad_proj, squares_all = lax.psum((proj_piece, squares), "dp")
    loss = squares_all / (row_count * lax.axis_size("dp"))
    return (hidden_acc, grad_proj, loss)


def solution(mesh):
    placed = (P("dp", "fsdp"), P("dp", "fsdp"), P("fsdp", None))
    return jax.shard_map(
        body,
        mesh=mesh,
        in_specs=placed,
        out_specs=(P("dp", "fsdp"), P("fsdp", None), P()),
        check_vma=False,
    )
```

profile of v0, /device:TPU:8, one launch (start us, length us, event | category | flops | bytes accessed | tf_op | source)
XLA Modules:
  0.0 944.8 jit_solution(3194999770944170075)
XLA Ops:
  7.2 0.0 copy-start
  7.2 0.0 copy-start.3
  7.2 0.0 reduce-scatter.2.cloned.1.call-start
  7.2 0.9 copy-done
  8.1 1.9 fusion.12
  10.0 0.0 reduce-scatter.2.cloned.1.call-update
  10.1 0.0 all-gather.2.cloned.1.call-start
  10.1 0.9 fusion.1
  11.1 229.4 %reduce-scatter.2.cloned.1.call-done = f32[96,128]{1,0:T(8,128)} async-done(((f32[1536,128]{1,0:T(8,128)}), f32[96,128]{1,0:T(8,128)}) %reduce-scatter.2.cloned.1.call-update) | async-done | bytes 49168 | tf_op jit(solution)/shard_map/reduce_scatter | solution.py:20
  240.5 0.8 multiply_reduce_fusion.1
  241.3 47.7 %all-reduce = (f32[128]{0:T(128)S(1)}, f32[128]{0:T(128)S(1)}) all-reduce(f32[128]{0:T(128)S(1)} %multiply_reduce_fusion.1, f32[128]{0:T(128)S(1)} %fusion.1), channel_id=1, replica_groups=mesh['dp'=32,'fsdp'=16] {'fsdp'}, use_global_device_ids=true, to_apply=%region_2.0 | all-reduce | flops 256 | bytes 2048 | tf_op jit(solution)/shard_map/psum | solution.py:27
  289.0 0.8 bitcast_convert_fusion
  289.8 0.1 copy.6
  289.9 0.0 copy-done.3
  289.9 0.1 fusion.10
  290.0 0.7 pad_maximum_fusion
  290.8 0.0 all-gather.2.cloned.1.call-update
  290.8 0.0 all-reduce.4.cloned.1.call-start
  290.9 61.7 %all-gather.2.cloned.1.call-done = bf16[4096,352]{1,0:T(8,128)(2,1)} async-done(((bf16[128,352]{1,0:T(8,128)(2,1)}), bf16[4096,352]{1,0:T(8,128)(2,1)}) %all-gather.2.cloned.1.call-update) | async-done | bytes 2883600 | tf_op jit(solution)/shard_map/all_gather | solution.py:36
  352.6 4.4 fusion.3
  357.0 0.0 copy-start.2
  357.0 0.0 all-reduce.4.cloned.1.call-update
  357.1 0.0 copy-start.4
  357.1 0.0 all-reduce.6.cloned.1.call-start
  357.1 205.8 %all-reduce.4.cloned.1.call-done = f32[128,4096]{1,0:T(8,128)} async-done(((f32[128,4096]{1,0:T(8,128)}), f32[128,4096]{1,0:T(8,128)}) %all-reduce.4.cloned.1.call-update) | async-done | bytes 2097168 | tf_op jit(solution)/shard_map/psum | solution.py:38
  562.9 0.0 copy-done.2
  562.9 0.0 copy-start.1
  562.9 3.5 fusion.5
  566.3 48.1 %psum.45 = f32[128]{0:T(128)S(1)} all-reduce(f32[128]{0:T(128)S(1)} %get-tuple-element.7), channel_id=1, replica_groups=mesh['dp'=32,'fsdp'=16] {'fsdp'}, use_global_device_ids=true, to_apply=%region_7.0 | all-reduce | flops 128 | bytes 1024 | tf_op jit(solution)/shard_map/psum | solution.py:11
  614.4 53.8 %all_gather.7 = bf16[128,1536]{0,1:T(8,128)(2,1)S(1)} all-gather(bf16[128,96]{0,1:T(8,128)(2,1)S(1)} %fusion.8), channel_id=1, replica_groups=mesh['dp'=32,'fsdp'=16] {'fsdp'}, dimensions={1}, use_global_device_ids=true | all-gather | bytes 417792 | tf_op jit(solution)/shard_map/all_gather | solution.py:48
  668.2 0.0 copy-done.4
  668.2 1.1 convolution_bitcast_fusion
  669.3 0.0 all-reduce.6.cloned.1.call-update
  669.3 0.0 copy-done.1
  669.3 1.1 multiply_reduce_fusion
  670.5 68.0 %psum.47 = f32[]{:T(128)} all-reduce(f32[]{:T(128)} %multiply_reduce_fusion), channel_id=1, replica_groups=mesh['dp'=32,'fsdp'=16] {'dp'}, use_global_device_ids=true, to_apply=%region_10.0 | all-reduce | flops 1 | bytes 8 | tf_op jit(solution)/shard_map/psum | solution.py:51
  739.2 0.9 fusion.13
  740.0 195.2 %all-reduce.6.cloned.1.call-done = f32[96,1536]{1,0:T(8,128)} async-done(((f32[96,1536]{1,0:T(8,128)}), f32[96,1536]{1,0:T(8,128)}) %all-reduce.6.cloned.1.call-update) | async-done | bytes 589840 | tf_op jit(solution)/shard_map/psum | solution.py:51
  935.2 1.9 copy.10
  (2 shorter events, 0.0 us)
Async XLA Ops:
  7.2 1.0 copy-start
  7.2 282.8 %copy-start.3 = (bf16[128,256]{1,0:T(8,128)(2,1)S(1)}, bf16[128,256]{1,0:T(8,128)(2,1)}, u32[]{:S(2)}) copy-start(bf16[128,256]{1,0:T(8,128)(2,1)} %param.4) | copy-start | bytes 196612
  7.2 233.3 %reduce-scatter.2.cloned.1.call-start = ((), (), s32[]{:S(2)}) async-start(), calls=%async_computation.1 | async-start | bytes 835584 | tf_op jit(solution)/shard_map/reduce_scatter | solution.py:20
  10.1 342.5 %all-gather.2.cloned.1.call-start = ((), (), s32[]{:S(2)}) async-start(), calls=%async_computation.2 | async-start | bytes 3244032 | tf_op jit(solution)/shard_map/all_gather | solution.py:36
  290.8 272.1 %all-reduce.4.cloned.1.call-start = ((), (), s32[]{:S(2)}) async-start(), calls=%async_computation.3 | async-start | bytes 4194304 | tf_op jit(solution)/shard_map/psum | solution.py:38
  357.0 205.8 %copy-start.2 = (f32[96,128]{1,0:T(8,128)S(1)}, f32[96,128]{1,0:T(8,128)}, u32[]{:S(2)}) copy-start(f32[96,128]{1,0:T(8,128)} %reduce-scatter.2.cloned.1.call-done) | copy-start | bytes 147460
  357.1 311.2 %copy-start.4 = (bf16[128,96]{0,1:T(8,128)(2,1)S(1)}, bf16[128,96]{0,1:T(8,128)(2,1)}, u32[]{:S(2)}) copy-start(bf16[128,96]{0,1:T(8,128)(2,1)} %param.3) | copy-start | bytes 73732
  357.1 578.1 %all-reduce.6.cloned.1.call-start = ((), (), s32[]{:S(2)}) async-start(), calls=%async_computation.4 | async-start | bytes 1179648 | tf_op jit(solution)/shard_map/psum | solution.py:51
  562.9 106.5 %copy-start.1 = (f32[128,4096]{1,0:T(8,128)S(1)}, f32[128,4096]{1,0:T(8,128)}, u32[]{:S(2)}) copy-start(f32[128,4096]{1,0:T(8,128)} %all-reduce.4.cloned.1.call-done) | copy-start | bytes 6291460
Sparse Core Ops, SparseCore 0:
  12.5 227.9 reduce-scatter.1
  290.9 61.6 all-gather.1
  357.2 205.6 all-reduce.3
  669.4 265.7 all-reduce.5
where the time goes:
time: 945 us
  waiting for transfers between devices  692 us (73%)
  blocking collectives  218 us (23%)
  between operations  15.6 us (2%)
  matrix products  11.7 us (1%)
    reduce_scatter x1, waiting for transfers between devices, body(): lax.psum_scatter(lax.dot_general(projector, hidden, width_cross, preferre...  229 us
    psum x1, waiting for transfers between devices, body(): differ = lax.psum(partial_value, 'fsdp')  206 us
    psum x1, waiting for transfers between devices, body(): grad_proj, squares_all = lax.psum((proj_piece, squares), 'dp')  195 us
    psum x1, blocking collectives, body(): grad_proj, squares_all = lax.psum((proj_piece, squares), 'dp')  68 us
    all_gather x1, waiting for transfers between devices, body(): lower_all = lax.all_gather(lower, 'dp', axis=0, tiled=True)  61.7 us
    all_gather x1, blocking collectives, body(): piece = lax.all_gather(grad_embed, 'fsdp', axis=1, tiled=True)  53.8 us
    psum x1, blocking collectives, radial_sum(): return lax.psum(jnp.sum(unit_f * grad_unit, axis=1), 'fsdp')  48.1 us
    psum x1, blocking collectives, body(): lax.psum((jnp.sum(embed * embed, axis=1), jnp.sum(teach_f * teach_f, axis...  47.7 us
  transfers between devices with their start and end apart: 4, of which 4 were waited for; matrix products, arithmetic and copies ran while one was open for 0% of the time, Pallas kernels for 0%

commit v1 on v0

--- a/solution.py
+++ b/solution.py
@@ -33,7 +33,9 @@
     target = (teach_f * lax.rsqrt(sq_teacher + EPSILON)[:, None]).astype(jnp.bfloat16)
     upper = jnp.concatenate([student, target], axis=1)
     lower = jnp.concatenate([student, -target], axis=1)
-    lower_all = lax.all_gather(lower, "dp", axis=0, tiled=True)
+    lower_all = jnp.concatenate(
+        lax.all_to_all(jnp.stack([lower] * lax.axis_size("dp"), axis=0), "dp", 0, 0), axis=0
+    )
     partial_value = lax.dot_general(upper, lower_all, contract, preferred_element_type=jnp.float32)
     differ = lax.psum(partial_value, "fsdp")
     squares = jnp.sum(differ * differ)

time: 945 us -> 950 us (level)
  blocking collectives: 218 us -> 290 us
  waiting for transfers between devices: 692 us -> 625 us
    all_to_all x0 -> x1, blocking collectives: none -> 72.2 us  [body(): lax.all_to_all(jnp.stack([lower] * lax.axis_size('dp'), axis=0), 'dp', 0, 0)]
    all_gather x1 -> x0, waiting for transfers between devices: 61.7 us -> none  [body(): lower_all = lax.all_gather(lower, 'dp', axis=0, tiled=True)]
  transfers between devices with their start and end apart: 4 -> 3, of which waited for: 4 -> 3; matrix products, arithmetic and copies ran while one was open for 0% -> 1% of each run, Pallas kernels for 0% -> 0%
where the time goes in v1:
time: 950 us
  waiting for transfers between devices  625 us (66%)
  blocking collectives  290 us (31%)
  between operations  15.6 us (2%)
    reduce_scatter x1, waiting for transfers between devices, body(): lax.psum_scatter(lax.dot_general(projector, hidden, width_cross, preferre...  229 us
    psum x1, waiting for transfers between devices, body(): differ = lax.psum(partial_value, 'fsdp')  201 us
    psum x1, waiting for transfers between devices, body(): grad_proj, squares_all = lax.psum((proj_piece, squares), 'dp')  195 us
    all_to_all x1, blocking collectives, body(): lax.all_to_all(jnp.stack([lower] * lax.axis_size('dp'), axis=0), 'dp', 0, 0)  72.2 us
    psum x1, blocking collectives, body(): grad_proj, squares_all = lax.psum((proj_piece, squares), 'dp')  68.1 us
    all_gather x1, blocking collectives, body(): piece = lax.all_gather(grad_embed, 'fsdp', axis=1, tiled=True)  53.9 us
    psum x1, blocking collectives, radial_sum(): return lax.psum(jnp.sum(unit_f * grad_unit, axis=1), 'fsdp')  48.1 us
    psum x1, blocking collectives, body(): lax.psum((jnp.sum(embed * embed, axis=1), jnp.sum(teach_f * teach_f, axis...  47.7 us
  transfers between devices with their start and end apart: 3, of which 3 were waited for; matrix products, arithmetic and copies ran while one was open for 1% of the time, Pallas kernels for 0%

profile of v1, /device:TPU:8, one launch (start us, length us, event | category | flops | bytes accessed | tf_op | source)
XLA Modules:
  0.0 949.9 jit_solution(17235194168977118549)
XLA Ops:
  7.2 0.0 copy-start
  7.2 0.0 reduce-scatter.2.cloned.1.call-start
  7.2 0.9 copy-done
  8.1 1.9 fusion.12
  10.0 0.0 reduce-scatter.2.cloned.1.call-update
  10.1 0.0 all-reduce.4.cloned.1.call-start
  10.1 0.9 fusion.1
  11.1 229.4 %reduce-scatter.2.cloned.1.call-done = f32[96,128]{1,0:T(8,128)} async-done(((f32[1536,128]{1,0:T(8,128)}), f32[96,128]{1,0:T(8,128)}) %reduce-scatter.2.cloned.1.call-update) | async-done | bytes 49168 | tf_op jit(solution)/shard_map/reduce_scatter | solution.py:20
  240.5 0.8 multiply_reduce_fusion.1
  241.3 47.7 %all-reduce = (f32[128]{0:T(128)S(1)}, f32[128]{0:T(128)S(1)}) all-reduce(f32[128]{0:T(128)S(1)} %multiply_reduce_fusion.1, f32[128]{0:T(128)S(1)} %fusion.1), channel_id=1, replica_groups=mesh['dp'=32,'fsdp'=16] {'fsdp'}, use_global_device_ids=true, to_apply=%region_2.0 | all-reduce | flops 256 | bytes 2048 | tf_op jit(solution)/shard_map/psum | solution.py:27
  289.0 0.8 bitcast_convert_fusion
  289.8 0.1 copy.11
  289.9 0.9 fusion.10
  290.9 0.1 pad_maximum_fusion
  291.0 0.1 copy.13
  291.1 0.4 stack.2
  291.5 72.2 %all_to_all.5 = bf16[32,128,352]{1,2,0:T(8,128)(2,1)S(1)} all-to-all(bf16[32,128,352]{1,2,0:T(8,128)(2,1)S(1)} %stack.2), channel_id=1, replica_groups=mesh['dp'=32,'fsdp'=16] {'dp'}, dimensions={0} | all-to-all | bytes 5767168 | tf_op jit(solution)/shard_map/all_to_all | solution.py:37
  363.7 2.1 fusion.3
  365.8 0.0 all-reduce.4.cloned.1.call-update
  365.8 0.0 copy-start.2
  365.8 0.0 all-reduce.6.cloned.1.call-start
  365.9 1.9 copy_bitcast_fusion
  367.8 0.0 copy-start.3
  367.8 200.8 %all-reduce.4.cloned.1.call-done = f32[128,4096]{1,0:T(8,128)} async-done(((f32[128,4096]{1,0:T(8,128)}), f32[128,4096]{1,0:T(8,128)}) %all-reduce.4.cloned.1.call-update) | async-done | bytes 2097168 | tf_op jit(solution)/shard_map/psum | solution.py:40
  568.6 0.0 copy-done.2
  568.7 0.0 copy-start.1
  568.7 3.2 fusion.5
  571.8 48.1 %psum.45 = f32[128]{0:T(128)S(1)} all-reduce(f32[128]{0:T(128)S(1)} %get-tuple-element.7), channel_id=1, replica_groups=mesh['dp'=32,'fsdp'=16] {'fsdp'}, use_global_device_ids=true, to_apply=%region_7.0 | all-reduce | flops 128 | bytes 1024 | tf_op jit(solution)/shard_map/psum | solution.py:11
  619.9 53.9 %all_gather.3 = bf16[128,1536]{0,1:T(8,128)(2,1)S(1)} all-gather(bf16[128,96]{0,1:T(8,128)(2,1)S(1)} %fusion.8), channel_id=1, replica_groups=mesh['dp'=32,'fsdp'=16] {'fsdp'}, dimensions={1}, use_global_device_ids=true | all-gather | bytes 417792 | tf_op jit(solution)/shard_map/all_gather | solution.py:50
  673.9 0.0 copy-done.3
  673.9 1.1 convolution_bitcast_fusion
  674.9 0.0 all-reduce.6.cloned.1.call-update
  675.0 0.0 copy-done.1
  675.0 1.1 multiply_reduce_fusion
  676.1 68.1 %psum.47 = f32[]{:T(128)} all-reduce(f32[]{:T(128)} %multiply_reduce_fusion), channel_id=1, replica_groups=mesh['dp'=32,'fsdp'=16] {'dp'}, use_global_device_ids=true, to_apply=%region_10.0 | all-reduce | flops 1 | bytes 8 | tf_op jit(solution)/shard_map/psum | solution.py:53
  744.9 0.9 fusion.13
  745.7 194.6 %all-reduce.6.cloned.1.call-done = f32[96,1536]{1,0:T(8,128)} async-done(((f32[96,1536]{1,0:T(8,128)}), f32[96,1536]{1,0:T(8,128)}) %all-reduce.6.cloned.1.call-update) | async-done | bytes 589840 | tf_op jit(solution)/shard_map/psum | solution.py:53
  940.3 1.9 copy.20
  (2 shorter events, 0.0 us)
Async XLA Ops:
  7.2 1.0 copy-start
  7.2 233.3 %reduce-scatter.2.cloned.1.call-start = ((), (), s32[]{:S(2)}) async-start(), calls=%async_computation.2 | async-start | bytes 835584 | tf_op jit(solution)/shard_map/reduce_scatter | solution.py:20
  10.1 558.6 %all-reduce.4.cloned.1.call-start = ((), (), s32[]{:S(2)}) async-start(), calls=%async_computation.3 | async-start | bytes 4194304 | tf_op jit(solution)/shard_map/psum | solution.py:40
  365.8 202.8 %copy-start.2 = (f32[96,128]{1,0:T(8,128)S(1)}, f32[96,128]{1,0:T(8,128)}, u32[]{:S(2)}) copy-start(f32[96,128]{1,0:T(8,128)} %reduce-scatter.2.cloned.1.call-done) | copy-start | bytes 147460
  365.8 574.5 %all-reduce.6.cloned.1.call-start = ((), (), s32[]{:S(2)}) async-start(), calls=%async_computation.4 | async-start | bytes 1179648 | tf_op jit(solution)/shard_map/psum | solution.py:53
  367.8 306.0 %copy-start.3 = (bf16[128,96]{0,1:T(8,128)(2,1)S(1)}, bf16[128,96]{0,1:T(8,128)(2,1)}, u32[]{:S(2)}) copy-start(bf16[128,96]{0,1:T(8,128)(2,1)} %param.3) | copy-start | bytes 73732
  568.7 106.3 %copy-start.1 = (f32[128,4096]{1,0:T(8,128)S(1)}, f32[128,4096]{1,0:T(8,128)}, u32[]{:S(2)}) copy-start(f32[128,4096]{1,0:T(8,128)} %all-reduce.4.cloned.1.call-done) | copy-start | bytes 6291460
Sparse Core Ops, SparseCore 0:
  12.5 227.9 reduce-scatter.1
  366.0 202.6 all-reduce.3
  675.1 265.1 all-reduce.5

commit v2 on v0

--- a/solution.py
+++ b/solution.py
@@ -35,7 +35,8 @@
     lower = jnp.concatenate([student, -target], axis=1)
     lower_all = lax.all_gather(lower, "dp", axis=0, tiled=True)
     partial_value = lax.dot_general(upper, lower_all, contract, preferred_element_type=jnp.float32)
-    differ = lax.psum(partial_value, "fsdp")
+    part_next = lax.all_gather(partial_value, "fsdp")
+    differ = jnp.sum(part_next, axis=0)
     squares = jnp.sum(differ * differ)
     grad_unit = 4.0 * jnp.dot(
         differ,

time: 945 us -> 1380 us (1.46)
  waiting for transfers between devices: 692 us -> 1120 us
    all_gather x0 -> x1, waiting for transfers between devices: none -> 627 us  [body(): part_next = lax.all_gather(partial_value, 'fsdp')]
    psum x1 -> x0, waiting for transfers between devices: 206 us -> none  [body(): differ = lax.psum(partial_value, 'fsdp')]
where the time goes in v2:
time: 1380 us
  waiting for transfers between devices  1120 us (81%)
  blocking collectives  213 us (15%)
  other arithmetic  16.3 us (1%)
  between operations  15.6 us (1%)
    all_gather x1, waiting for transfers between devices, body(): part_next = lax.all_gather(partial_value, 'fsdp')  627 us
    reduce_scatter x1, waiting for transfers between devices, body(): lax.psum_scatter(lax.dot_general(projector, hidden, width_cross, preferre...  229 us
    psum x1, waiting for transfers between devices, body(): grad_proj, squares_all = lax.psum((proj_piece, squares), 'dp')  198 us
    psum x1, blocking collectives, body(): grad_proj, squares_all = lax.psum((proj_piece, squares), 'dp')  68.1 us
    all_gather x1, waiting for transfers between devices, body(): lower_all = lax.all_gather(lower, 'dp', axis=0, tiled=True)  61.8 us
    all_gather x1, blocking collectives, body(): piece = lax.all_gather(grad_embed, 'fsdp', axis=1, tiled=True)  49.2 us
    psum x1, blocking collectives, radial_sum(): return lax.psum(jnp.sum(unit_f * grad_unit, axis=1), 'fsdp')  48.2 us
    psum x1, blocking collectives, body(): lax.psum((jnp.sum(embed * embed, axis=1), jnp.sum(teach_f * teach_f, axis...  47.7 us
  transfers between devices with their start and end apart: 4, of which 4 were waited for; matrix products, arithmetic and copies ran while one was open for 0% of the time, Pallas kernels for 0%

profile of v2, /device:TPU:8, one launch (start us, length us, event | category | flops | bytes accessed | tf_op | source)
XLA Modules:
  0.0 1375.6 jit_solution(9857784370625576216)
XLA Ops:
  7.2 0.0 copy-start
  7.2 0.0 copy-start.2
  7.2 0.0 reduce-scatter.2.cloned.1.call-start
  7.2 0.9 copy-done
  8.1 1.9 fusion.12
  10.0 0.0 reduce-scatter.2.cloned.1.call-update
  10.1 0.0 all-gather.4.cloned.1.call-start
  10.1 0.9 fusion.1
  11.1 229.4 %reduce-scatter.2.cloned.1.call-done = f32[96,128]{1,0:T(8,128)} async-done(((f32[1536,128]{1,0:T(8,128)}), f32[96,128]{1,0:T(8,128)}) %reduce-scatter.2.cloned.1.call-update) | async-done | bytes 49168 | tf_op jit(solution)/shard_map/reduce_scatter | solution.py:20
  240.5 0.8 multiply_reduce_fusion.1
  241.3 47.7 %all-reduce = (f32[128]{0:T(128)S(1)}, f32[128]{0:T(128)S(1)}) all-reduce(f32[128]{0:T(128)S(1)} %multiply_reduce_fusion.1, f32[128]{0:T(128)S(1)} %fusion.1), channel_id=1, replica_groups=mesh['dp'=32,'fsdp'=16] {'fsdp'}, use_global_device_ids=true, to_apply=%region_2.0 | all-reduce | flops 256 | bytes 2048 | tf_op jit(solution)/shard_map/psum | solution.py:27
  289.0 0.8 bitcast_convert_fusion
  289.8 0.1 copy.8
  289.9 0.0 copy-done.2
  289.9 0.1 fusion.10
  290.0 0.7 pad_maximum_fusion
  290.8 0.0 all-gather.4.cloned.1.call-update
  290.8 0.0 all-gather.6.cloned.1.call-start
  290.9 61.8 %all-gather.4.cloned.1.call-done = bf16[4096,352]{1,0:T(8,128)(2,1)} async-done(((bf16[128,352]{1,0:T(8,128)(2,1)}), bf16[4096,352]{1,0:T(8,128)(2,1)}) %all-gather.4.cloned.1.call-update) | async-done | bytes 2883600 | tf_op jit(solution)/shard_map/all_gather | solution.py:36
  352.6 4.4 fusion.3
  357.0 0.0 all-gather.6.cloned.1.call-update
  357.1 0.0 all-reduce.3.cloned.1.call-start
  357.1 627.0 %all-gather.6.cloned.1.call-done = f32[2048,4096]{1,0:T(8,128)} async-done(((f32[128,4096]{1,0:T(8,128)}), f32[2048,4096]{1,0:T(8,128)}) %all-gather.6.cloned.1.call-update) | async-done | bytes 33554448 | tf_op jit(solution)/shard_map/all_gather | solution.py:38
  984.1 0.0 copy-start.1
  984.1 11.8 reduce_sum.47
  995.9 0.0 copy-done.1
  995.9 0.0 copy-start.3
  995.9 2.7 fusion.5
  998.6 48.2 %psum.37 = f32[128]{0:T(128)S(1)} all-reduce(f32[128]{0:T(128)S(1)} %get-tuple-element.7), channel_id=1, replica_groups=mesh['dp'=32,'fsdp'=16] {'fsdp'}, use_global_device_ids=true, to_apply=%region_7.0 | all-reduce | flops 128 | bytes 1024 | tf_op jit(solution)/shard_map/psum | solution.py:11
  1046.7 49.2 %all_gather.15 = bf16[128,1536]{0,1:T(8,128)(2,1)S(1)} all-gather(bf16[128,96]{0,1:T(8,128)(2,1)S(1)} %fusion.8), channel_id=1, replica_groups=mesh['dp'=32,'fsdp'=16] {'fsdp'}, dimensions={1}, use_global_device_ids=true | all-gather | bytes 417792 | tf_op jit(solution)/shard_map/all_gather | solution.py:49
  1096.0 0.0 copy-done.3
  1096.0 1.1 convolution_bitcast_fusion
  1097.1 0.0 all-reduce.3.cloned.1.call-update
  1097.1 1.1 multiply_reduce_fusion
  1098.2 68.1 %psum.39 = f32[]{:T(128)} all-reduce(f32[]{:T(128)} %multiply_reduce_fusion), channel_id=1, replica_groups=mesh['dp'=32,'fsdp'=16] {'dp'}, use_global_device_ids=true, to_apply=%region_10.0 | all-reduce | flops 1 | bytes 8 | tf_op jit(solution)/shard_map/psum | solution.py:52
  1167.0 0.9 fusion.13
  1167.8 198.2 %all-reduce.3.cloned.1.call-done = f32[96,1536]{1,0:T(8,128)} async-done(((f32[96,1536]{1,0:T(8,128)}), f32[96,1536]{1,0:T(8,128)}) %all-reduce.3.cloned.1.call-update) | async-done | bytes 589840 | tf_op jit(solution)/shard_map/psum | solution.py:52
  1366.0 1.9 copy.11
  (2 shorter events, 0.0 us)
Async XLA Ops:
  7.2 1.0 copy-start
  7.2 282.8 %copy-start.2 = (bf16[128,256]{1,0:T(8,128)(2,1)S(1)}, bf16[128,256]{1,0:T(8,128)(2,1)}, u32[]{:S(2)}) copy-start(bf16[128,256]{1,0:T(8,128)(2,1)} %param.4) | copy-start | bytes 196612
  7.2 233.3 %reduce-scatter.2.cloned.1.call-start = ((), (), s32[]{:S(2)}) async-start(), calls=%async_computation.1 | async-start | bytes 835584 | tf_op jit(solution)/shard_map/reduce_scatter | solution.py:20
  10.1 342.5 %all-gather.4.cloned.1.call-start = ((), (), s32[]{:S(2)}) async-start(), calls=%async_computation.2 | async-start | bytes 3244032 | tf_op jit(solution)/shard_map/all_gather | solution.py:36
  290.8 693.3 %all-gather.6.cloned.1.call-start = ((), (), s32[]{:S(2)}) async-start(), calls=%async_computation.4 | async-start | bytes 35651584 | tf_op jit(solution)/shard_map/all_gather | solution.py:38
  357.1 1008.9 %all-reduce.3.cloned.1.call-start = ((), (), s32[]{:S(2)}) async-start(), calls=%async_computation.3 | async-start | bytes 1179648 | tf_op jit(solution)/shard_map/psum | solution.py:52
  984.1 11.8 copy-start.1
  995.9 100.1 %copy-start.3 = (bf16[128,96]{0,1:T(8,128)(2,1)S(1)}, bf16[128,96]{0,1:T(8,128)(2,1)}, u32[]{:S(2)}) copy-start(bf16[128,96]{0,1:T(8,128)(2,1)} %param.3) | copy-start | bytes 73732
Sparse Core Ops, SparseCore 0:
  12.5 227.9 reduce-scatter.1
  290.9 61.6 all-gather.3
  357.2 626.8 all-gather.5
  1097.2 268.7 all-reduce.2
